TPU v7x, 256 devices: a whole 4x4x8 slice. The times are simulated.
256 devices in a mesh: grid: 64 (over z, y, core), layer: 4 (over x).
Axes of the slice: x: 4, y: 4, z: 8, core: 2. Of those that a mesh axis runs over, the one named last changes fastest.
Arguments:
- x_blocks: bfloat16 [4096, 128, 128], P('grid'), may hold values from -0.3984375 to 0.3984375
- send_first: int32 [64, 4, 64, 1], P('grid', 'layer'), may hold values from 0 to 63
- send_left: int32 [64, 4, 64, 1], P('grid', 'layer'), may hold values from 0 to 63
- send_right: int32 [64, 64, 1], P('grid'), may hold values from 0 to 63
- terms_first: int32 [4096, 4, 12, 2], P('grid', 'layer'), may hold values from 0 to 63
- terms_second: int32 [4096, 4, 12, 2], P('grid', 'layer'), may hold values from 0 to 63
- live_first: int32 [4096, 4], P('grid', 'layer'), may hold values from 1 to 12, as said below
- live_second: int32 [4096, 4], P('grid', 'layer'), may hold values from 1 to 12, as said below
Outputs:
- square: bfloat16 [4096, 128, 128], P('grid', 'layer')
- sign_step: bfloat16 [4096, 128, 128], P('grid', 'layer')
Inputs may be any that keep to these rules, and one draw needn't show every extreme that they name: `live_first`: number of live term slots of an output block on one layer; later slots are unused. `live_second`: number of live term slots of an output block on one layer; later slots are unused.
All inputs are finite; a program needn't handle non-finite values.
Results may differ from a plain program's by a relative error of at most 0.015.
Values may be sent and summed in bfloat16 or wider, within the bound.
A program may use at most 128 MiB of HBM per device.

v0:
```python
import jax
import jax.numpy as jnp
from jax import lax
from jax.sharding import PartitionSpec as P


def block_product(left_buffer, right_buffer, terms, live):
    block_count = terms.shape[0]
    term_slots = terms.shape[1]
    group_size = 16
    term_groups = terms.reshape(block_count // group_size, group_size, term_slots, 2)
    live_groups = live.reshape(block_count // group_size, group_size)

    def one_group(packed):
        term_pair, alive_count = packed
        keep_mask = (
            lax.broadcasted_iota(jnp.int32, (group_size, term_slots), 1) < alive_count[:, None]
        ).astype(jnp.bfloat16)
        left_stack = left_buffer[term_pair[:, :, 0]] * keep_mask[:, :, None, None]
        right_stack = right_buffer[term_pair[:, :, 1]]
        return jnp.einsum(
            "gtij,gtjk->gik", left_stack, right_stack, preferred_element_type=jnp.float32
        )

    result = lax.map(one_group, (term_groups, live_groups))
    return result.reshape(block_count, left_buffer.shape[1], right_buffer.shape[2])


def local(
    x_blocks, send_first, send_left, send_right, terms_first, terms_second, live_first, live_second
):
    peer_count = lax.axis_size("grid")
    layers = lax.axis_size("layer")
    block_width = x_blocks.shape[1]
    share_rows = block_width // layers
    row_start = lax.axis_index("layer") * share_rows
    first_slots = send_first.reshape(peer_count, -1)
    left_slots = send_left.reshape(peer_count, -1)
    right_slots = send_right.reshape(peer_count, -1)
    first_got = lax.all_to_all(
        x_blocks[first_slots], "grid", split_axis=0, concat_axis=0, tiled=True
    )
    first_buffer = first_got.reshape(-1, block_width, block_width)
    first_terms = terms_first.reshape(terms_first.shape[0], terms_first.shape[2], 2)
    partial_value = block_product(first_buffer, first_buffer, first_terms, live_first.reshape(-1))
    rounded_partial = partial_value.astype(jnp.bfloat16)
    layer_total = lax.psum(rounded_partial, "layer").astype(jnp.float32).astype(jnp.bfloat16)
    square = lax.dynamic_slice_in_dim(layer_total, row_start, share_rows, 1)
    right_got = lax.all_to_all(
        layer_total[right_slots], "grid", split_axis=0, concat_axis=0, tiled=True
    )
    left_got = lax.all_to_all(x_blocks[left_slots], "grid", split_axis=0, concat_axis=0, tiled=True)
    second_terms = terms_second.reshape(terms_second.shape[0], terms_second.shape[2], 2)
    update = block_product(
        left_got.reshape(-1, block_width, block_width),
        right_got.reshape(-1, block_width, block_width),
        second_terms,
        live_second.reshape(-1),
    )
    update_share = lax.psum_scatter(
        update.astype(jnp.bfloat16), "layer", scatter_dimension=1, tiled=True
    ).astype(jnp.float32)
    own_rows = lax.dynamic_slice_in_dim(x_blocks, row_start, share_rows, 1).astype(jnp.float32)
    sign_step = (1.5 * own_rows - 0.5 * update_share).astype(jnp.bfloat16)
    return (square, sign_step)


def solution(mesh):
    return jax.shard_map(
        local,
        mesh=mesh,
        in_specs=(
            P("grid", None, None),
            P("grid", "layer", None, None),
            P("grid", "layer", None, None),
            P("grid", None, None),
            P("grid", "layer", None, None),
            P("grid", "layer", None, None),
            P("grid", "layer"),
            P("grid", "layer"),
        ),
        out_specs=(P("grid", "layer", None), P("grid", "layer", None)),
        check_vma=False,
    )
```

profile of v0, /device:TPU:1, one launch (start us, length us, event | category | flops | bytes accessed | tf_op | source)
XLA Modules:
  0.0 448.8 jit_solution(10415710490538978905)
XLA Ops:
  11.6 13.3 %all-to-all-start = ((bf16[64,1,128,128]{3,2,1,0:T(8,128)(2,1)}), bf16[64,1,128,128]{3,2,1,0:T(8,128)(2,1)S(1)}, u32[]{:S(2)}, u32[]{:S(2)}) async-start(bf16[64,1,128,128]{3,2,1,0:T(8,128)(2,1)} %bitcast.90), calls=%async_computation | async-start | bytes 4194304 | tf_op jit(solution)/shard_map/all_to_all | solution.py:40
  30.0 44.6 %all-to-all-done = bf16[64,1,128,128]{3,2,1,0:T(8,128)(2,1)S(1)} async-done(((bf16[64,1,128,128]{3,2,1,0:T(8,128)(2,1)}), bf16[64,1,128,128]{3,2,1,0:T(8,128)(2,1)S(1)}, u32[]{:S(2)}, u32[]{:S(2)}) %all-to-all-start) | async-done | bytes 2097184 | tf_op jit(solution)/shard_map/all_to_all | solution.py:40
  83.7 95.1 %while.20 = (s32[]{:T(128)}, bf16[4,16,128,128]{3,2,1,0:T(8,128)(2,1)}, s32[4,16,12,2]{1,0,3,2:T(4,128)S(1)}, bf16[64,128,128]{2,1,0:T(8,128)(2,1)S(1)}, s32[4,16]{1,0:T(4,128)S(1)}, /*index=5*/s32[]{:T(128)}) while((s32[]{:T(128)}, bf16[4,16,128,128]{3,2,1,0:T(8,128)(2,1)}, s32[4,16,12,2]{1,0,3,2:T(4,128)S(1)}, ...), condition=%wide.region_1.2_spmd, body=%wide.region_0.1_spmd.sunk | while | flops 808455680 | bytes 38821912 | solution.py:25
  84.1 8.1 %gather_fusion = bf16[192,128,128]{2,1,0:T(8,128)(2,1)} fusion(bf16[64,128,128]{2,1,0:T(8,128)(2,1)S(1)} %get-tuple-element.204, s32[1024]{0:T(1024)S(1)} %pad_clamp_fusion.11), kind=kCustom, calls=%fused_computation.1.clone.1 | custom fusion | bytes 12583680 | tf_op jit(solution)/shard_map/while/body/eval_jaxpr/gather | solution.py:20
  92.1 8.0 %gather_fusion.1 = bf16[192,128,128]{2,1,0:T(8,128)(2,1)} fusion(bf16[64,128,128]{2,1,0:T(8,128)(2,1)S(1)} %get-tuple-element.204, s32[1024]{0:T(1024)S(1)} %pad_clamp_fusion.12), kind=kCustom, calls=%fused_computation.clone.1 | custom fusion | bytes 12583680 | tf_op jit(solution)/shard_map/while/body/eval_jaxpr/gather | solution.py:19
  107.8 8.1 %gather_fusion = bf16[192,128,128]{2,1,0:T(8,128)(2,1)} fusion(bf16[64,128,128]{2,1,0:T(8,128)(2,1)S(1)} %get-tuple-element.204, s32[1024]{0:T(1024)S(1)} %pad_clamp_fusion.11), kind=kCustom, calls=%fused_computation.1.clone.1 | custom fusion | bytes 12583680 | tf_op jit(solution)/shard_map/while/body/eval_jaxpr/gather | solution.py:20
  115.9 8.1 %gather_fusion.1 = bf16[192,128,128]{2,1,0:T(8,128)(2,1)} fusion(bf16[64,128,128]{2,1,0:T(8,128)(2,1)S(1)} %get-tuple-element.204, s32[1024]{0:T(1024)S(1)} %pad_clamp_fusion.12), kind=kCustom, calls=%fused_computation.clone.1 | custom fusion | bytes 12583680 | tf_op jit(solution)/shard_map/while/body/eval_jaxpr/gather | solution.py:19
  131.6 8.1 %gather_fusion = bf16[192,128,128]{2,1,0:T(8,128)(2,1)} fusion(bf16[64,128,128]{2,1,0:T(8,128)(2,1)S(1)} %get-tuple-element.204, s32[1024]{0:T(1024)S(1)} %pad_clamp_fusion.11), kind=kCustom, calls=%fused_computation.1.clone.1 | custom fusion | bytes 12583680 | tf_op jit(solution)/shard_map/while/body/eval_jaxpr/gather | solution.py:20
  139.7 8.0 %gather_fusion.1 = bf16[192,128,128]{2,1,0:T(8,128)(2,1)} fusion(bf16[64,128,128]{2,1,0:T(8,128)(2,1)S(1)} %get-tuple-element.204, s32[1024]{0:T(1024)S(1)} %pad_clamp_fusion.12), kind=kCustom, calls=%fused_computation.clone.1 | custom fusion | bytes 12583680 | tf_op jit(solution)/shard_map/while/body/eval_jaxpr/gather | solution.py:19
  155.4 8.1 %gather_fusion = bf16[192,128,128]{2,1,0:T(8,128)(2,1)} fusion(bf16[64,128,128]{2,1,0:T(8,128)(2,1)S(1)} %get-tuple-element.204, s32[1024]{0:T(1024)S(1)} %pad_clamp_fusion.11), kind=kCustom, calls=%fused_computation.1.clone.1 | custom fusion | bytes 12583680 | tf_op jit(solution)/shard_map/while/body/eval_jaxpr/gather | solution.py:20
  163.4 8.0 %gather_fusion.1 = bf16[192,128,128]{2,1,0:T(8,128)(2,1)} fusion(bf16[64,128,128]{2,1,0:T(8,128)(2,1)S(1)} %get-tuple-element.204, s32[1024]{0:T(1024)S(1)} %pad_clamp_fusion.12), kind=kCustom, calls=%fused_computation.clone.1 | custom fusion | bytes 12583680 | tf_op jit(solution)/shard_map/while/body/eval_jaxpr/gather | solution.py:19
  179.4 64.2 %all-reduce.2.cloned.1.call-done = bf16[64,128,128]{2,1,0:T(8,128)(2,1)} async-done(((bf16[64,128,128]{2,1,0:T(8,128)(2,1)}), bf16[64,128,128]{2,1,0:T(8,128)(2,1)}) %all-reduce.2.cloned.1.call-update) | async-done | bytes 2097168 | tf_op jit(solution)/shard_map/psum | solution.py:47
  247.4 10.8 %all-to-all-start.2 = ((bf16[64,1,128,128]{3,2,1,0:T(8,128)(2,1)}), bf16[64,1,128,128]{3,2,1,0:T(8,128)(2,1)S(1)}, u32[]{:S(2)}, u32[]{:S(2)}) async-start(bf16[64,1,128,128]{3,2,1,0:T(8,128)(2,1)} %bitcast.89), calls=%async_computation.2 | async-start | bytes 4194304 | tf_op jit(solution)/shard_map/all_to_all | solution.py:49
  259.3 48.6 %all-to-all-done.2 = bf16[64,1,128,128]{3,2,1,0:T(8,128)(2,1)S(1)} async-done(((bf16[64,1,128,128]{3,2,1,0:T(8,128)(2,1)}), bf16[64,1,128,128]{3,2,1,0:T(8,128)(2,1)S(1)}, u32[]{:S(2)}, u32[]{:S(2)}) %all-to-all-start.2) | async-done | bytes 2097184 | tf_op jit(solution)/shard_map/all_to_all | solution.py:49
  309.7 101.5 %while.21 = (s32[]{:T(128)}, bf16[4,16,128,128]{3,2,1,0:T(8,128)(2,1)}, s32[4,16,12,2]{1,0,3,2:T(4,128)S(1)}, bf16[64,128,128]{2,1,0:T(8,128)(2,1)}, s32[4,16]{1...) while((s32[]{:T(128)}, bf16[4,16,128,128]{3,2,1,0:T(8,128)(2,1)}, ...), condition=%wide.region_4.5_spmd, body=%wide.region_3.4_spmd.sunk | while | flops 808455680 | bytes 38821920 | solution.py:25
  310.1 8.1 %gather_fusion.2 = bf16[192,128,128]{2,1,0:T(8,128)(2,1)} fusion(bf16[64,128,128]{2,1,0:T(8,128)(2,1)S(1)} %get-tuple-element.226, s32[1024]{0:T(1024)S(1)} %pad_clamp_fusion.13), kind=kCustom, calls=%fused_computation.3.clone.1 | custom fusion | bytes 12583680 | tf_op jit(solution)/shard_map/while/body/eval_jaxpr/gather | solution.py:20
  318.2 9.6 %gather_fusion.3 = bf16[192,128,128]{2,1,0:T(8,128)(2,1)} fusion(bf16[64,128,128]{2,1,0:T(8,128)(2,1)} %get-tuple-element.224, s32[1024]{0:T(1024)S(1)} %pad_clamp_fusion.14), kind=kCustom, calls=%fused_computation.2.clone.1 | custom fusion | bytes 12583680 | tf_op jit(solution)/shard_map/while/body/eval_jaxpr/gather | solution.py:19
  335.5 8.1 %gather_fusion.2 = bf16[192,128,128]{2,1,0:T(8,128)(2,1)} fusion(bf16[64,128,128]{2,1,0:T(8,128)(2,1)S(1)} %get-tuple-element.226, s32[1024]{0:T(1024)S(1)} %pad_clamp_fusion.13), kind=kCustom, calls=%fused_computation.3.clone.1 | custom fusion | bytes 12583680 | tf_op jit(solution)/shard_map/while/body/eval_jaxpr/gather | solution.py:20
  343.5 9.6 %gather_fusion.3 = bf16[192,128,128]{2,1,0:T(8,128)(2,1)} fusion(bf16[64,128,128]{2,1,0:T(8,128)(2,1)} %get-tuple-element.224, s32[1024]{0:T(1024)S(1)} %pad_clamp_fusion.14), kind=kCustom, calls=%fused_computation.2.clone.1 | custom fusion | bytes 12583680 | tf_op jit(solution)/shard_map/while/body/eval_jaxpr/gather | solution.py:19
  360.8 8.1 %gather_fusion.2 = bf16[192,128,128]{2,1,0:T(8,128)(2,1)} fusion(bf16[64,128,128]{2,1,0:T(8,128)(2,1)S(1)} %get-tuple-element.226, s32[1024]{0:T(1024)S(1)} %pad_clamp_fusion.13), kind=kCustom, calls=%fused_computation.3.clone.1 | custom fusion | bytes 12583680 | tf_op jit(solution)/shard_map/while/body/eval_jaxpr/gather | solution.py:20
  368.9 9.6 %gather_fusion.3 = bf16[192,128,128]{2,1,0:T(8,128)(2,1)} fusion(bf16[64,128,128]{2,1,0:T(8,128)(2,1)} %get-tuple-element.224, s32[1024]{0:T(1024)S(1)} %pad_clamp_fusion.14), kind=kCustom, calls=%fused_computation.2.clone.1 | custom fusion | bytes 12583680 | tf_op jit(solution)/shard_map/while/body/eval_jaxpr/gather | solution.py:19
  386.2 8.1 %gather_fusion.2 = bf16[192,128,128]{2,1,0:T(8,128)(2,1)} fusion(bf16[64,128,128]{2,1,0:T(8,128)(2,1)S(1)} %get-tuple-element.226, s32[1024]{0:T(1024)S(1)} %pad_clamp_fusion.13), kind=kCustom, calls=%fused_computation.3.clone.1 | custom fusion | bytes 12583680 | tf_op jit(solution)/shard_map/while/body/eval_jaxpr/gather | solution.py:20
  394.3 9.6 %gather_fusion.3 = bf16[192,128,128]{2,1,0:T(8,128)(2,1)} fusion(bf16[64,128,128]{2,1,0:T(8,128)(2,1)} %get-tuple-element.224, s32[1024]{0:T(1024)S(1)} %pad_clamp_fusion.14), kind=kCustom, calls=%fused_computation.2.clone.1 | custom fusion | bytes 12583680 | tf_op jit(solution)/shard_map/while/body/eval_jaxpr/gather | solution.py:19
  413.1 26.6 %reduce-scatter.2.cloned.1.call-done = bf16[64,32,128]{2,1,0:T(8,128)(2,1)} async-done(((bf16[64,128,128]{2,1,0:T(8,128)(2,1)}), bf16[64,32,128]{2,1,0:T(8,128)(2,1)}) %reduce-scatter.2.cloned.1.call-update) | async-done | bytes 524304 | tf_op jit(solution)/shard_map/reduce_scatter | solution.py:60
  (115 shorter events, 91.1 us)
Async XLA Ops:
  11.6 13.8 %copy-start.2 = (s32[64,1]{0,1:T(1,128)S(1)}, s32[64,1]{0,1:T(1,128)}, u32[]{:S(2)}) copy-start(s32[64,1]{0,1:T(1,128)} %param.18) | copy-start | bytes 772
  11.6 14.6 %copy-start = (s32[64,1,12,2]{0,3,2,1:T(2,128)S(1)}, s32[64,1,12,2]{0,3,2,1:T(2,128)}, u32[]{:S(2)}) copy-start(s32[64,1,12,2]{0,3,2,1:T(2,128)} %param.16) | copy-start | bytes 18436
  11.6 63.0 %all-to-all-start = ((bf16[64,1,128,128]{3,2,1,0:T(8,128)(2,1)}), bf16[64,1,128,128]{3,2,1,0:T(8,128)(2,1)S(1)}, u32[]{:S(2)}, u32[]{:S(2)}) async-start(bf16[64,1,128,128]{3,2,1,0:T(8,128)(2,1)} %bitcast.90), calls=%async_computation | async-start | bytes 4194304 | tf_op jit(solution)/shard_map/all_to_all | solution.py:40
  74.6 172.8 %all-to-all-start.1 = ((bf16[64,1,128,128]{3,2,1,0:T(8,128)(2,1)}), bf16[64,1,128,128]{3,2,1,0:T(8,128)(2,1)}, u32[]{:S(2)}, u32[]{:S(2)}) async-start(bf16[64,1,128,128]{3,2,1,0:T(8,128)(2,1)} %bitcast.88), calls=%async_computation.1 | async-start | bytes 4194304 | tf_op jit(solution)/shard_map/all_to_all | solution.py:52
  81.8 161.9 %all-reduce.2.cloned.1.call-start = ((), (), s32[]{:S(2)}) async-start(), calls=%async_computation.4 | async-start | bytes 4194304 | tf_op jit(solution)/shard_map/psum | solution.py:47
  178.7 0.7 copy-start.3
  247.4 11.1 %copy-start.4 = (s32[64,1]{0,1:T(1,128)S(1)}, s32[64,1]{0,1:T(1,128)}, u32[]{:S(2)}) copy-start(s32[64,1]{0,1:T(1,128)} %param.19) | copy-start | bytes 772
  247.4 11.8 %copy-start.1 = (s32[64,1,12,2]{0,3,2,1:T(2,128)S(1)}, s32[64,1,12,2]{0,3,2,1:T(2,128)}, u32[]{:S(2)}) copy-start(s32[64,1,12,2]{0,3,2,1:T(2,128)} %param.17) | copy-start | bytes 18436
  247.4 60.5 %all-to-all-start.2 = ((bf16[64,1,128,128]{3,2,1,0:T(8,128)(2,1)}), bf16[64,1,128,128]{3,2,1,0:T(8,128)(2,1)S(1)}, u32[]{:S(2)}, u32[]{:S(2)}) async-start(bf16[64,1,128,128]{3,2,1,0:T(8,128)(2,1)} %bitcast.89), calls=%async_computation.2 | async-start | bytes 4194304 | tf_op jit(solution)/shard_map/all_to_all | solution.py:49
  258.2 181.5 %reduce-scatter.2.cloned.1.call-start = ((), (), s32[]{:S(2)}) async-start(), calls=%async_computation.5 | async-start | bytes 2621440 | tf_op jit(solution)/shard_map/reduce_scatter | solution.py:60
Sparse Core Ops, SparseCore 0:
  178.9 64.7 all-reduce.1
  411.3 28.3 reduce-scatter.1
where the time goes:
time: 450 us; the launch traced here: 449 us
  waiting for transfers between devices  184 us (41%)
  local copies, waits for them, and re-layouts  156 us (35%)
  matrix products  58.1 us (13%)
  starting transfers between devices  31.6 us (7%)
  between operations  14.1 us (3%)
  other arithmetic  4.99 us (1%)
    gather x8, local copies, waits for them, and re-layouts, one_group(): left_stack = left_buffer[term_pair[:, :, 0]] * keep_mask[:, :, None, None]  70.7 us
    gather x8, local copies, waits for them, and re-layouts, one_group(): right_stack = right_buffer[term_pair[:, :, 1]]  64.5 us
    psum x1, waiting for transfers between devices, local(): lax.psum(rounded_partial, 'layer').astype(jnp.float32).astype(jnp.bfloat16)  64.2 us
    dot_general x8, matrix products, one_group(): jnp.einsum('gtij,gtjk->gik', left_stack, right_stack, preferred_element_t...  58.1 us
    all_to_all x1, waiting for transfers between devices, local(): lax.all_to_all(layer_total[right_slots], 'grid', split_axis=0, concat_axi...  48.6 us
    all_to_all x1, waiting for transfers between devices, local(): lax.all_to_all(x_blocks[first_slots], 'grid', split_axis=0, concat_axis=0...  44.6 us
    reduce_scatter x1, waiting for transfers between devices, local(): lax.psum_scatter(update.astype(jnp.bfloat16), 'layer', scatter_dimension=...  26.6 us
    all_to_all x1, starting transfers between devices, local(): lax.all_to_all(x_blocks[first_slots], 'grid', split_axis=0, concat_axis=0...  13.3 us
  transfers between devices with their start and end apart: 5, of which 4 were waited for; matrix products, arithmetic and copies ran while one was open for 24% of the time, Pallas kernels for 0%

commit v1 on v0

v1 whole, which is shorter than its diff:
```python
import functools

import jax
import jax.numpy as jnp
from jax import lax
from jax.experimental import pallas as pl
from jax.experimental.pallas import tpu as pltpu
from jax.sharding import PartitionSpec as P

MESH = pl.DeviceIdType.MESH
BF = jnp.bfloat16
F32 = jnp.float32
HALF = 64
CHUNKS = 4
ROWS = 16


def kernel(
    grid_n,
    y_n,
    blocks,
    terms,
    idx_ref,
    tab_ref,
    x_ref,
    sq_ref,
    out_ref,
    stage,
    lstage,
    rstage,
    first,
    left,
    right,
    part,
    part2,
    rs1,
    rs2,
    comb1,
    comb2,
    tabs,
    stab,
    send_sem,
    recv_sem,
    tab_send,
    tab_recv,
    loc_sem,
    rs_send,
    rs_recv,
):
    me = lax.axis_index("grid")
    lay = lax.axis_index("layer")
    width = x_ref.shape[1]
    quarter = width // 4
    z_n = grid_n // (2 * y_n)
    z, y, core = me // (2 * y_n), (me // 2) % y_n, me % 2
    per = blocks // CHUNKS

    def peer(i):
        dz, m = ((i % z_n) * 5) % z_n, i // z_n
        dy, dc = m // 2, m % 2
        return ((z + dz) % z_n) * (2 * y_n) + ((y + dy) % y_n) * 2 + (core + dc) % 2

    barrier = pltpu.get_barrier_semaphore()

    def greet(i, carry):
        pl.semaphore_signal(barrier, inc=1, device_id=(peer(i), lay), device_id_type=MESH)
        return carry

    lax.fori_loop(1, grid_n, greet, 0)
    for step in range(1, 4):
        pl.semaphore_signal(
            barrier, inc=1, device_id=(me, (lay + step) % 4), device_id_type=MESH
        )

    def fill_first(i, carry):
        stage[i] = x_ref[idx_ref[terms, peer(i)]]
        return carry

    lax.fori_loop(0, grid_n, fill_first, 0)
    first[me] = stage[0]
    first[grid_n] = jnp.zeros((width, width), BF)
    left[grid_n] = jnp.zeros((width, width), BF)
    tabs[lay] = tab_ref[...]
    pl.semaphore_wait(barrier, grid_n - 1 + 3)

    def tab_copy(step):
        return pltpu.make_async_remote_copy(
            src_ref=tab_ref,
            dst_ref=tabs.at[lay],
            send_sem=tab_send.at[step - 1],
            recv_sem=tab_recv.at[step - 1],
            device_id=(me, (lay + step) % 4),
            device_id_type=MESH,
        )

    for step in range(1, 4):
        tab_copy(step).start()

    def spread(src, dst, which):
        def one(i, carry):
            pltpu.make_async_remote_copy(
                src_ref=src.at[i],
                dst_ref=dst.at[me],
                send_sem=send_sem.at[which],
                recv_sem=recv_sem.at[which],
                device_id=(peer(i), lay),
                device_id_type=MESH,
            ).start()
            return carry

        lax.fori_loop(1, grid_n, one, 0)

    def wait_all(src, sem):
        whole = src.at[pl.ds(1, grid_n - 1)]
        pltpu.make_async_copy(whole, whole, sem).wait()

    spread(stage, first, 0)

    for step in range(1, 4):
        tab_copy(step).wait_recv()
    to_smem = pltpu.make_async_copy(tabs, stab, loc_sem)
    to_smem.start()
    to_smem.wait()

    lane = lax.broadcasted_iota(jnp.int32, (width, width), 1) // quarter
    sub = lax.broadcasted_iota(jnp.int32, (width, width), 0)
    lane_all = lax.broadcasted_iota(jnp.int32, (width, width), 1)
    picks = [
        ((sub == lay * quarter + lane_all - j * quarter) & (lane == j)).astype(BF)
        for j in range(4)
    ]
    pick = jnp.concatenate(picks, axis=0)

    def fill_left(i, carry):
        d = peer(i)
        rows = jnp.concatenate([x_ref[stab[j, terms, d]] for j in range(4)], axis=1)
        lstage[i] = jnp.dot(rows, pick, preferred_element_type=F32).astype(BF)
        return carry

    lax.fori_loop(0, grid_n, fill_left, 0)
    left[me] = lstage[0]
    wait_all(stage, send_sem.at[0])
    spread(lstage, left, 1)
    wait_all(stage, recv_sem.at[0])

    right_lay, left_lay, far_lay = (lay + 1) % 4, (lay + 3) % 4, (lay + 2) % 4

    def rows_of(q, h):
        return pl.ds(pl.multiple_of(q * quarter + h * ROWS, ROWS), ROWS)

    def reduce_rows(phase, product, src, got, comb, finish):
        def copy(kind, c):
            span = pl.ds(c * per, per)
            if kind == 0:
                ref, to = src.at[span, rows_of(far_lay, 0)], right_lay
            elif kind == 1:
                ref, to = src.at[span, rows_of(far_lay, 1)], left_lay
            elif kind == 2:
                ref, to = src.at[span, rows_of(right_lay, 1)], right_lay
            elif kind == 3:
                ref, to = src.at[span, rows_of(left_lay, 0)], left_lay
            elif kind == 4:
                ref, to = comb.at[0, span], right_lay
            else:
                ref, to = comb.at[1, span], left_lay
            return pltpu.make_async_remote_copy(
                src_ref=ref,
                dst_ref=got.at[kind, span],
                send_sem=rs_send.at[phase, kind, c],
                recv_sem=rs_recv.at[phase, kind, c],
                device_id=(me, to),
                device_id_type=MESH,
            )

        def relay(c):
            span = pl.ds(c * per, per)
            for kind, q in ((0, right_lay), (1, left_lay)):
                copy(kind, c).wait_recv()
                own = src[span, rows_of(q, kind)].astype(F32)
                comb[kind, span] = (own + got[kind, span].astype(F32)).astype(BF)
                copy(4 + kind, c).start()

        def chunk(c, carry):
            def one(o, inner):
                product(o)
                return inner

            lax.fori_loop(c * per, (c + 1) * per, one, 0)
            for kind in range(4):
                copy(kind, c).start()

            @pl.when(c >= 1)
            def _():
                relay(c - 1)

            return carry

        lax.fori_loop(0, CHUNKS, chunk, 0)
        relay(CHUNKS - 1)

        def close(c, carry):
            span = pl.ds(c * per, per)
            for h, direct, joined in ((0, 3, 4), (1, 2, 5)):
                copy(direct, c).wait_recv()
                copy(joined, c).wait_recv()
                total = (
                    src[span, rows_of(lay, h)].astype(F32)
                    + got[direct, span].astype(F32)
                    + got[joined, span].astype(F32)
                )
                finish(span, h, total)
            return carry

        lax.fori_loop(0, CHUNKS, close, 0)

        def drain(c, carry):
            for kind in range(6):
                copy(kind, c).wait_send()
            return carry

        return drain

    def product_first(o):
        acc = jnp.zeros((width, width), F32)
        for t in range(0, terms, 2):
            a = jnp.concatenate([first[idx_ref[u, o]] for u in (t, t + 1)], axis=1)
            b = jnp.concatenate([first[idx_ref[u, HALF + o]] for u in (t, t + 1)], axis=0)
            acc = acc + jnp.dot(a, b, preferred_element_type=F32)
        part[o] = acc.astype(BF)

    def finish_first(span, h, total):
        sq_ref[span, pl.ds(h * ROWS, ROWS)] = total.astype(BF)

    drain_first = reduce_rows(0, product_first, part, rs1, comb1, finish_first)

    def fill_right(i, carry):
        rstage[i] = sq_ref[idx_ref[terms, HALF + peer(i)]]
        return carry

    lax.fori_loop(0, grid_n, fill_right, 0)
    right[me] = rstage[0]
    spread(rstage, right, 2)
    wait_all(lstage, recv_sem.at[1])
    wait_all(rstage, recv_sem.at[2])

    def product_second(o):
        acc = jnp.zeros((width, width), F32)
        for t in range(0, terms, 2):
            a_parts, b_parts = [], []
            for u in (t, t + 1):
                lefts = [left[stab[j, u, o]] for j in range(4)]
                low = jnp.where(lane == 0, lefts[0], lefts[1])
                high = jnp.where(lane == 2, lefts[2], lefts[3])
                a_parts.append(jnp.where(lane < 2, low, high))
                b_parts += [right[stab[j, u, HALF + o]] for j in range(4)]
            a = jnp.concatenate(a_parts, axis=1)
            b = jnp.concatenate(b_parts, axis=0)
            acc = acc + jnp.dot(a, b, preferred_element_type=F32)
        part2[o] = acc.astype(BF)

    def finish_second(span, h, total):
        own = x_ref[span, rows_of(lay, h)].astype(F32)
        out_ref[span, pl.ds(h * ROWS, ROWS)] = (1.5 * own - 0.5 * total).astype(BF)

    drain_second = reduce_rows(1, product_second, part2, rs2, comb2, finish_second)

    lax.fori_loop(0, CHUNKS, drain_first, 0)
    lax.fori_loop(0, CHUNKS, drain_second, 0)
    for step in range(1, 4):
        tab_copy(step).wait_send()
    wait_all(lstage, send_sem.at[1])
    wait_all(rstage, send_sem.at[2])


def term_table(terms, live, extra, slots):
    blocks, count = terms.shape[0], terms.shape[2]
    pairs = terms.reshape(blocks, count, 2)
    keep = lax.broadcasted_iota(jnp.int32, (blocks, count), 1) < live.reshape(blocks, 1)
    lefts = jnp.where(keep, pairs[:, :, 0], slots)
    rows = jnp.stack([lefts, pairs[:, :, 1]], axis=0)
    rows = jnp.pad(rows.transpose(2, 0, 1), ((0, 0), (0, 0), (0, HALF - blocks)))
    table = jnp.concatenate([rows.reshape(count, 2 * HALF), extra.reshape(1, 2 * HALF)], axis=0)
    return jnp.pad(table, ((0, 16 - count - 1), (0, 0)))


def local(
    y_n,
    x_blocks,
    send_first,
    send_left,
    send_right,
    terms_first,
    terms_second,
    live_first,
    live_second,
):
    grid_n = lax.axis_size("grid")
    blocks, width = x_blocks.shape[0], x_blocks.shape[1]
    count = terms_first.shape[2]
    quarter = width // 4

    def padded(slots):
        flat = slots.reshape(-1)
        return jnp.pad(flat, (0, HALF - flat.shape[0]))

    extra_first = jnp.concatenate([padded(send_first), padded(send_right)])
    extra_second = jnp.concatenate([padded(send_left), padded(send_left)])
    idx = term_table(terms_first, live_first, extra_first, grid_n)
    tab = term_table(terms_second, live_second, extra_second, grid_n)
    share = jax.ShapeDtypeStruct((blocks, quarter, width), BF)
    vmem = pl.BlockSpec(memory_space=pltpu.VMEM)
    dma = pltpu.SemaphoreType.DMA
    return pl.pallas_call(
        functools.partial(kernel, grid_n, y_n, blocks, count),
        out_shape=(share, share),
        in_specs=[pl.BlockSpec(memory_space=pltpu.SMEM), vmem, vmem],
        out_specs=(vmem, vmem),
        scratch_shapes=[
            pltpu.VMEM((grid_n, width, width), BF),
            pltpu.VMEM((grid_n, width, width), BF),
            pltpu.VMEM((grid_n, quarter, width), BF),
            pltpu.VMEM((grid_n + 1, width, width), BF),
            pltpu.VMEM((grid_n + 1, width, width), BF),
            pltpu.VMEM((grid_n, quarter, width), BF),
            pltpu.VMEM((blocks, width, width), BF),
            pltpu.VMEM((blocks, width, width), BF),
            pltpu.VMEM((6, blocks, ROWS, width), BF),
            pltpu.VMEM((6, blocks, ROWS, width), BF),
            pltpu.VMEM((2, blocks, ROWS, width), BF),
            pltpu.VMEM((2, blocks, ROWS, width), BF),
            pltpu.VMEM((4, 16, 128), jnp.int32),
            pltpu.SMEM((4, 16, 128), jnp.int32),
            dma((3,)),
            dma((3,)),
            dma((3,)),
            dma((3,)),
            dma,
            dma((2, 6, CHUNKS)),
            dma((2, 6, CHUNKS)),
        ],
        compiler_params=pltpu.CompilerParams(
            collective_id=0, has_side_effects=True, vmem_limit_bytes=48 * 1024 * 1024
        ),
    )(idx, tab, x_blocks)


def solution(mesh, y_n=4):
    return jax.shard_map(
        functools.partial(local, y_n),
        mesh=mesh,
        in_specs=(
            P("grid", None, None),
            P("grid", "layer", None, None),
            P("grid", "layer", None, None),
            P("grid", None, None),
            P("grid", "layer", None, None),
            P("grid", "layer", None, None),
            P("grid", "layer"),
            P("grid", "layer"),
        ),
        out_specs=(P("grid", "layer", None), P("grid", "layer", None)),
        check_vma=False,
    )
```

time: 450 us -> 159 us (0.35)
  waiting for transfers between devices: 184 us -> 0 us
  local copies, waits for them, and re-layouts: 156 us -> 4.78 us
  Pallas kernels: 0 us -> 150 us
  matrix products: 58.1 us -> 0 us
  starting transfers between devices: 31.6 us -> 0 us
  between operations: 14.1 us -> 0.67 us
    pallas_call x0 -> x1, Pallas kernels: none -> 150 us  [local(): pl.pallas_call(functools.partial(kernel, grid_n, y_n, blocks, count), out...]
    gather x19 -> x0, local copies, waits for them, and re-layouts: 146 us -> none  [the longest x8 70.7 us: one_group(): left_stack = left_buffer[term_pair[:, :, 0]] * keep_mask[:, :, None, None]]
    all_to_all x3 -> x0, waiting for transfers between devices: 93.2 us -> none  [the longest x1 48.6 us: local(): lax.all_to_all(layer_total[right_slots], 'grid', split_axis=0, concat_axi...]
    psum x1 -> x0, waiting for transfers between devices: 64.2 us -> none  [local(): lax.psum(rounded_partial, 'layer').astype(jnp.float32).astype(jnp.bfloat16)]
    dot_general x8 -> x0, matrix products: 58.1 us -> none  [one_group(): jnp.einsum('gtij,gtjk->gik', left_stack, right_stack, preferred_element_t...]
    all_to_all x3 -> x0, starting transfers between devices: 31.3 us -> none  [the longest x1 13.3 us: local(): lax.all_to_all(x_blocks[first_slots], 'grid', split_axis=0, concat_axis=0...]
    reduce_scatter x1 -> x0, waiting for transfers between devices: 26.6 us -> none  [local(): lax.psum_scatter(update.astype(jnp.bfloat16), 'layer', scatter_dimension=...]
  transfers between devices with their start and end apart: 5 -> 0, of which waited for: 4 -> 0; matrix products, arithmetic and copies ran while one was open for 24% -> 0% of each run, Pallas kernels for 0% -> 0%
where the time goes in v1:
time: 159 us; the launch traced here: 158 us
  Pallas kernels  150 us (94%)
  local copies, waits for them, and re-layouts  4.78 us (3%)
  other arithmetic  3.04 us (2%)
    pallas_call x1, Pallas kernels, local(): pl.pallas_call(functools.partial(kernel, grid_n, y_n, blocks, count), out...  150 us

profile of v1, /device:TPU:1, one launch (start us, length us, event | category | flops | bytes accessed | tf_op | source)
XLA Modules:
  0.0 158.1 jit_solution(2807223422219709087)
XLA Ops:
  0.6 0.7 add_bitcast_fusion.2
  1.4 0.8 add_bitcast_fusion.3
  2.2 0.7 slice_bitcast_fusion.2
  2.9 0.7 compare_select_fusion.1
  3.6 0.1 reshape.123
  3.7 0.7 slice_bitcast_fusion
  4.5 0.7 compare_select_fusion
  5.2 0.1 reshape.128
  5.3 0.0 copy-start
  5.3 1.6 %copy-done = bf16[64,128,128]{2,1,0:T(8,128)(2,1)S(1)} copy-done((bf16[64,128,128]{2,1,0:T(8,128)(2,1)S(1)}, bf16[64,128,128]{2,1,0:T(8,128)(2,1)}, u32[]{:S(2)}) %copy-start) | copy-done | bytes 2097176
  6.9 149.6 %shard_map.95 = (bf16[64,32,128]{2,1,0:T(8,128)(2,1)S(1)}, bf16[64,32,128]{2,1,0:T(8,128)(2,1)S(1)}) custom-call(s32[16,128]{1,0:T(8,128)S(1)} %pad.7.idx_ref, s32[16,128]{1,0:T(8,128)S(1)} %pad.8.tab_ref, bf16[64,128,128]{2,1,0:T(8,128)(2,1)S(1)} %copy-done), custom_call_target="tpu_custom_call" | custom-call | tf_op jit(solution)/shard_map/pallas_call | solution.py:313
  156.5 0.8 copy.12
  157.3 0.8 copy.13
  (6 shorter events, 0.1 us)
Async XLA Ops:
  5.3 1.6 %copy-start = (bf16[64,128,128]{2,1,0:T(8,128)(2,1)S(1)}, bf16[64,128,128]{2,1,0:T(8,128)(2,1)}, u32[]{:S(2)}) copy-start(bf16[64,128,128]{2,1,0:T(8,128)(2,1)} %x_ref.1) | copy-start | bytes 6291460

commit v2 on v1

v2 whole, which is shorter than its diff:
```python
import functools

import jax
import jax.numpy as jnp
from jax import lax
from jax.experimental import pallas as pl
from jax.experimental.pallas import tpu as pltpu
from jax.sharding import PartitionSpec as P

MESH = pl.DeviceIdType.MESH
BF = jnp.bfloat16
F32 = jnp.float32
HALF = 64
CHUNKS = 8
LAG = 2
FAR_FIRST = (4, 3, 5, 2, 6, 1, 7)
ROWS = 16
SUBS = 2


def slot_order(k, n):
    k = k % n
    return 0 if k == 0 else (2 * k - 1 if 2 * k <= n else 2 * (n - k))


def kernel(
    grid_n,
    y_n,
    blocks,
    terms,
    x_hbm,
    sf_ref,
    sl_ref,
    ssr,
    tf_ref,
    ts_ref,
    lf_ref,
    ls_ref,
    sq_ref,
    out_ref,
    x_ref,
    *refs,
):
    near_n = 2 * (grid_n // (2 * y_n) // 4) + 1
    gathered = refs[:near_n]
    run(
        grid_n, y_n, blocks, terms, x_hbm, sf_ref, sl_ref, ssr, tf_ref, ts_ref, lf_ref, ls_ref,
        sq_ref, out_ref, x_ref, gathered, *refs[near_n:]
    )


def run(
    grid_n,
    y_n,
    blocks,
    terms,
    x_hbm,
    sf_ref,
    sl_ref,
    ssr,
    tf_ref,
    ts_ref,
    lf_ref,
    ls_ref,
    sq_ref,
    out_ref,
    x_ref,
    gathered,
    stage,
    lstage,
    far_out,
    far_in,
    lfar_out,
    lfar_in,
    mid,
    rstage,
    first,
    left,
    right,
    part,
    part2,
    rs1,
    rs2,
    comb1,
    comb2,
    ftab,
    sftab,
    tabs,
    stab,
    rows,
    srows,
    send_sem,
    recv_sem,
    ring_send,
    ring_recv,
    far_send,
    far_recv,
    cross_send,
    cross_recv,
    tab_send,
    tab_recv,
    row_send,
    row_recv,
    loc_sem,
    rs_send,
    rs_recv,
):
    me = lax.axis_index("grid")
    lay = lax.axis_index("layer")
    load_x = pltpu.make_async_copy(x_hbm, x_ref, loc_sem.at[0])
    load_x.start()
    width = x_ref.shape[1]
    quarter = width // 4
    z_n = grid_n // (2 * y_n)
    yc_n = 2 * y_n
    z, y, core = me // yc_n, (me // 2) % y_n, me % 2
    yc = y * 2 + core
    per = blocks // CHUNKS
    sub = blocks // SUBS
    plane_n = yc_n * 4
    half_z = z_n // 2
    reach = half_z // 2
    half_plane = plane_n // 2
    zs = [lax.rem(z + dz, z_n) * yc_n for dz in range(z_n)]
    lays = [lax.rem(lay + dx, 4) for dx in range(4)]

    def mate_yc(m):
        return lax.rem(y + lax.div(m, 2), y_n) * 2 + lax.rem(core + m, 2)

    def at_z(dz):
        return (zs[dz % z_n] + yc, lay)

    def each_peer(act):
        def one(m, carry):
            other = mate_yc(m)
            for dz in FAR_FIRST:
                if 0 < dz < z_n:
                    act(m * z_n + dz, zs[dz] + other)

            @pl.when(m > 0)
            def _():
                act(m * z_n, zs[0] + other)

            return carry

        lax.fori_loop(0, yc_n, one, 0)

    def each_mate(low, high, act):
        def one(m, carry):
            d = zs[0] + mate_yc(m)
            for dx in range(1, 4):
                act(m * 4 + dx, d, lays[dx])

            @pl.when(m > 0)
            def _():
                act(m * 4, d, lay)

            return carry

        lax.fori_loop(low, high, one, 0)

    my_rows = pl.ds(pl.multiple_of(lay * quarter, quarter), quarter)

    barrier = pltpu.get_barrier_semaphore()

    def greet(d, to):
        pl.semaphore_signal(barrier, inc=1, device_id=(d, to), device_id_type=MESH)

    each_peer(lambda i, d: greet(d, lay))

    def greet_layers(m, carry):
        d = zs[0] + mate_yc(m)
        for dx in range(1, 4):
            greet(d, lays[dx])
        return carry

    lax.fori_loop(0, yc_n, greet_layers, 0)

    def moved(slots):
        away = lax.rem(lax.div(slots, yc_n) - z + z_n, z_n)
        order = jnp.where(2 * away <= z_n, 2 * away - 1, 2 * (z_n - away))
        order = jnp.where(away == 0, 0, order)
        return lax.rem(slots, yc_n), order

    def pad_row(values):
        return jnp.pad(values, ((0, 0), (0, HALF - values.shape[1])))

    term = lax.broadcasted_iota(jnp.int32, (terms, 1, blocks), 0)
    span_o = pl.ds(0, blocks)
    for table, live, to in ((tf_ref, lf_ref, ftab), (ts_ref, ls_ref, tabs.at[lay])):
        keep = term < live[...].reshape(1, 1, blocks)
        to[...] = jnp.zeros(to.shape, jnp.int32)
        lefts, rights = table[:, pl.ds(0, 1)], table[:, pl.ds(1, 1)]
        at_yc, order = moved(lefts)
        if to is ftab:
            lefts = at_yc * z_n + order
            at_yc, order = moved(rights)
            rights = at_yc * z_n + order
        else:
            lefts = order * yc_n + at_yc
        to[:, pl.ds(0, 1), span_o] = jnp.where(keep, lefts, grid_n)
        to[:, pl.ds(1, 1), span_o] = rights
    rows[0, lay] = jnp.concatenate([pad_row(sf_ref[...]), pad_row(sl_ref[...])], axis=1)
    first[grid_n] = jnp.zeros((width, width), BF)
    left[grid_n] = jnp.zeros((width, width), BF)
    load_x.wait()
    gathered[0][...] = x_ref[:, my_rows, :]
    pl.semaphore_wait(barrier, grid_n - 1 + 3 * yc_n)

    def hop(up, k, s):
        if k == 1:
            src = 0
        else:
            src = slot_order(-(k - 1) if up else k - 1, z_n)
        dst = slot_order(-k if up else k, z_n)
        span = pl.ds(s * sub, sub)
        which = 0 if up else 1
        return pltpu.make_async_remote_copy(
            src_ref=gathered[src].at[span],
            dst_ref=gathered[dst].at[span],
            send_sem=ring_send.at[which, k - 1, s],
            recv_sem=ring_recv.at[which, k - 1, s],
            device_id=at_z(1 if up else -1),
            device_id_type=MESH,
        )

    def hops():
        return [(up, s) for s in range(SUBS) for up in (True, False)]

    def tab_copy(step):
        return pltpu.make_async_remote_copy(
            src_ref=tabs.at[lay],
            dst_ref=tabs.at[lay],
            send_sem=tab_send.at[step - 1],
            recv_sem=tab_recv.at[step - 1],
            device_id=(me, lays[step]),
            device_id_type=MESH,
        )

    def row_copy(step):
        return pltpu.make_async_remote_copy(
            src_ref=rows.at[0, lay],
            dst_ref=rows.at[0, lay],
            send_sem=row_send.at[step - 1],
            recv_sem=row_recv.at[step - 1],
            device_id=(me, lays[step]),
            device_id_type=MESH,
        )

    def rows_copy(step):
        return pltpu.make_async_remote_copy(
            src_ref=rows.at[0],
            dst_ref=rows.at[slot_order(-step, z_n)],
            send_sem=row_send.at[2 + step % z_n],
            recv_sem=row_recv.at[2 + step % z_n],
            device_id=at_z(step),
            device_id_type=MESH,
        )

    for step in range(1, 4):
        row_copy(step).start()
    for up, s in hops():
        hop(up, 1, s).start()
    for step in range(1, 4):
        tab_copy(step).start()
    for step in range(1, 4):
        row_copy(step).wait_recv()
    near = [step for k in range(1, reach + 1) for step in (k, -k)]
    for step in near:
        rows_copy(step).start()
    for step in near:
        rows_copy(step).wait_recv()
    for step in range(1, 4):
        tab_copy(step).wait_recv()
    moves = [
        pltpu.make_async_copy(rows, srows, loc_sem.at[0]),
        pltpu.make_async_copy(tabs, stab, loc_sem.at[1]),
        pltpu.make_async_copy(ftab, sftab, loc_sem.at[2]),
    ]
    for move in moves:
        move.start()
    for move in moves:
        move.wait()

    def group(k):
        if k == 0:
            return 0, 1
        return 2 * k - 1, 2

    def plane_copy(src, dst, which, low, count, d, to):
        return pltpu.make_async_remote_copy(
            src_ref=src,
            dst_ref=dst.at[pl.ds(yc * z_n + low, count), my_rows],
            send_sem=send_sem.at[which],
            recv_sem=recv_sem.at[which],
            device_id=(d, to),
            device_id_type=MESH,
        )

    def plane_send(src, dst, which, k):
        low, count = group(k)

        def one(i, d, to):
            plane_copy(src.at[i, pl.ds(low, count)], dst, which, low, count, d, to).start()

        each_mate(0, yc_n, one)
        dst[pl.ds(yc * z_n + low, count), my_rows] = src[0, pl.ds(low, count)]

    def left_direct(k):
        low, count = group(k)
        for r in range(low, low + count):
            slots = pl.ds(r * yc_n + yc, 1)

            def one(i, d, to):
                pltpu.make_async_remote_copy(
                    src_ref=lstage.at[i, pl.ds(r, 1)],
                    dst_ref=left.at[slots, my_rows],
                    send_sem=send_sem.at[1],
                    recv_sem=recv_sem.at[1],
                    device_id=(d, to),
                    device_id_type=MESH,
                ).start()

            each_mate(0, yc_n, one)
            left[slots, my_rows] = lstage[0, pl.ds(r, 1)]

    def left_across(piece, src_of):
        slot = piece * yc_n + yc

        def one(m, carry):
            pltpu.make_async_remote_copy(
                src_ref=src_of(m),
                dst_ref=mid.at[:, slot],
                send_sem=send_sem.at[3],
                recv_sem=recv_sem.at[3],
                device_id=(zs[0] + mate_yc(m), lay),
                device_id_type=MESH,
            ).start()
            return carry

        lax.fori_loop(1, yc_n, one, 0)
        mid[:, slot] = src_of(0)[...]

    def cross_copy(dx):
        return pltpu.make_async_remote_copy(
            src_ref=mid.at[dx],
            dst_ref=left.at[pl.ds(mid_low, mid_n), my_rows],
            send_sem=cross_send.at[dx - 1],
            recv_sem=cross_recv.at[dx - 1],
            device_id=(me, lays[dx]),
            device_id_type=MESH,
        )

    def first_picks(r, d, put):
        for dx in range(4):
            put(dx, gathered[r][srows[r, lays[dx], 0, d]])

    lane_q = lax.broadcasted_iota(jnp.int32, (quarter, width), 1) // quarter

    def swap(a, b, groups):
        w = groups * quarter
        low = (lane_q // groups) % 2 == 0
        return (
            jnp.where(low, a, pltpu.roll(b, w, 1)),
            jnp.where(low, pltpu.roll(a, width - w, 1), b),
        )

    backs = [lax.rem(q - lay + 4, 4) for q in range(4)]

    def left_picks(r, d, put):
        p0, p1, p2, p3 = [
            gathered[r][srows[r, j, 0, HALF + d]].astype(F32) for j in range(4)
        ]
        t0, t2 = swap(p0, p2, 2)
        t1, t3 = swap(p1, p3, 2)
        q0, q1 = swap(t0, t1, 1)
        q2, q3 = swap(t2, t3, 1)
        for q, piece in enumerate((q0, q1, q2, q3)):
            put(backs[q], piece.astype(BF))

    def fill_group(picks, dst, k):
        low, count = group(k)

        def one(m, carry):
            d = zs[0] + mate_yc(m)
            for r in range(low, low + count):

                def put(dx, value):
                    dst[m * 4 + dx, r] = value

                picks(r, d, put)
            return carry

        lax.fori_loop(0, yc_n, one, 0)

    whole_steps = list(range(1, half_z - reach))
    far_n = 2 * len(whole_steps) + 1
    far_low = 2 * reach + 1
    last_step = half_z - reach

    def far_parts():
        out = [(last_step, 0)]
        for e in whole_steps:
            out += [(e, 0), (e, 1)]
        return out

    def fill_far(picks, dst, seg):
        e, h = far_parts()[seg]
        for up in (True, False):
            r = slot_order(-reach if up else reach, z_n)
            which = 0 if up else 1
            span = h if e < last_step else which

            def one(m, carry):
                d = zs[(e if up else -e) % z_n] + mate_yc(m)

                def put(dx, value):
                    dst[which, e - 1, m * 4 + dx] = value

                picks(r, d, put)
                return carry

            lax.fori_loop(span * (yc_n // 2), (span + 1) * (yc_n // 2), one, 0)

    def far_copy(src, dst, kind, up, seg):
        e, h = far_parts()[seg]
        which = 0 if up else 1
        span = pl.ds((h if e < last_step else which) * half_plane, half_plane)
        slot = slot_order(-(reach + e) if up else reach + e, z_n) - far_low
        return pltpu.make_async_remote_copy(
            src_ref=src.at[which, e - 1, span],
            dst_ref=dst.at[slot, span],
            send_sem=far_send.at[kind, which, seg],
            recv_sem=far_recv.at[kind, which, seg],
            device_id=at_z(e if up else -e),
            device_id_type=MESH,
        )

    def far_plane_send(src, dst, which, low, count, m_low, m_high):
        def one(i, d, to):
            piece = src.at[pl.ds(low, count), i]
            plane_copy(piece, dst, which, far_low + low, count, d, to).start()

        each_mate(m_low, m_high, one)
        if m_low == 0:
            dst[pl.ds(yc * z_n + far_low + low, count), my_rows] = src[pl.ds(low, count), 0]

    def arrive(k):
        for up, s in hops():
            hop(up, k, s).wait_recv()
            if k < reach:
                hop(up, k + 1, s).start()

    both = (True, False)
    parts = range(len(far_parts()))
    for k in range(0, reach + 1):
        if k > 0:
            arrive(k)
        if k == reach:
            for seg in parts:
                fill_far(first_picks, far_out, seg)
                for up in both:
                    far_copy(far_out, far_in, 0, up, seg).start()
        fill_group(first_picks, stage, k)
        plane_send(stage, first, 0, k)
        fill_group(left_picks, lstage, k)
        if k < reach:
            left_direct(k)
    for seg in parts:
        fill_far(left_picks, lfar_out, seg)
    for seg in parts:
        for up in both:
            far_copy(far_out, far_in, 0, up, seg).wait_recv()
        if seg == 0:
            far_plane_send(far_in, first, 0, far_n - 1, 1, 0, yc_n)
        else:
            e, h = far_parts()[seg]
            half = yc_n // 2
            far_plane_send(far_in, first, 0, 2 * e - 2, 2, h * half, (h + 1) * half)
    for seg in parts:
        for up in both:
            far_copy(lfar_out, lfar_in, 1, up, seg).start()
    near_pieces = 2 * reach - 1
    mid_low = near_pieces * yc_n
    mid_n = grid_n - mid_low
    for r in (0, 1):
        left_across(r, lambda m, r=r: lstage.at[pl.ds(m * 4, 4), near_pieces + r])

    def wait_all(src, sem):
        whole = src.at[pl.ds(1, src.shape[0] - 1)]
        pltpu.make_async_copy(whole, whole, sem).wait()

    def wait_plane(dst, sem):
        whole = dst.at[pl.ds(0, (plane_n - 1) * z_n // 4)]
        pltpu.make_async_copy(whole, whole, sem).wait()

    wait_plane(first, recv_sem.at[0])

    right_lay, left_lay, far_lay = lays[1], lays[3], lays[2]

    def rows_of(q, h):
        return pl.ds(pl.multiple_of(q * quarter + h * ROWS, ROWS), ROWS)

    def reduce_rows(phase, together, product, src, got, comb, between, finish):
        def copy(kind, c):
            span = pl.ds(c * per, per)
            if kind == 0:
                ref, to = src.at[span, rows_of(far_lay, 0)], right_lay
            elif kind == 1:
                ref, to = src.at[span, rows_of(far_lay, 1)], left_lay
            elif kind == 2:
                ref, to = src.at[span, rows_of(right_lay, 1)], right_lay
            elif kind == 3:
                ref, to = src.at[span, rows_of(left_lay, 0)], left_lay
            elif kind == 4:
                ref, to = comb.at[0, span], right_lay
            else:
                ref, to = comb.at[1, span], left_lay
            return pltpu.make_async_remote_copy(
                src_ref=ref,
                dst_ref=got.at[kind, span],
                send_sem=rs_send.at[phase, kind, c],
                recv_sem=rs_recv.at[phase, kind, c],
                device_id=(me, to),
                device_id_type=MESH,
            )

        def relay(c):
            span = pl.ds(c * per, per)
            for kind, q in ((0, right_lay), (1, left_lay)):
                copy(kind, c).wait_recv()
                own = src[span, rows_of(q, kind)].astype(F32)
                comb[kind, span] = (own + got[kind, span].astype(F32)).astype(BF)
                copy(4 + kind, c).start()

        def chunk(c, carry):
            def some(i, inner):
                for n in range(together):
                    product(c * per + i * together + n)
                return inner

            lax.fori_loop(0, per // together, some, 0)
            for kind in range(4):
                copy(kind, c).start()

            @pl.when(c >= LAG)
            def _():
                relay(c - LAG)

            return carry

        lax.fori_loop(0, CHUNKS, chunk, 0)
        between()
        for c in range(CHUNKS - LAG, CHUNKS):
            relay(c)

        def close(c, carry):
            span = pl.ds(c * per, per)
            for h, direct, joined in ((0, 3, 4), (1, 2, 5)):
                copy(direct, c).wait_recv()
                copy(joined, c).wait_recv()
                total = (
                    src[span, rows_of(lay, h)].astype(F32)
                    + got[direct, span].astype(F32)
                    + got[joined, span].astype(F32)
                )
                finish(span, h, total)
            return carry

        lax.fori_loop(0, CHUNKS, close, 0)

        def drain(c, carry):
            for kind in range(6):
                copy(kind, c).wait_send()
            return carry

        return drain

    def product_first(o):
        acc = jnp.zeros((width, width), F32)
        for t in range(0, terms, 2):
            a = jnp.concatenate([first[sftab[u, 0, o]] for u in (t, t + 1)], axis=1)
            b = jnp.concatenate([first[sftab[u, 1, o]] for u in (t, t + 1)], axis=0)
            acc = acc + jnp.dot(a, b, preferred_element_type=F32)
        part[o] = acc.astype(BF)

    def finish_first(span, h, total):
        sq_ref[span, pl.ds(h * ROWS, ROWS)] = total.astype(BF)

    def send_late():
        for seg in parts:
            for up in both:
                far_copy(lfar_out, lfar_in, 1, up, seg).wait_recv()
        for f in range(far_n):
            left_across(2 + f, lambda m, f=f: lfar_in.at[f, pl.ds(m * 4, 4)])

    drain_first = reduce_rows(0, 4, product_first, part, rs1, comb1, send_late, finish_first)

    def fill_right(i, d):
        rstage[i] = sq_ref[ssr[0, d]]

    rstage[0] = sq_ref[ssr[0, me]]
    each_peer(fill_right)
    right[me] = rstage[0]

    def send_right(i, d):
        pltpu.make_async_remote_copy(
            src_ref=rstage.at[i],
            dst_ref=right.at[me],
            send_sem=send_sem.at[2],
            recv_sem=recv_sem.at[2],
            device_id=(d, lay),
            device_id_type=MESH,
        ).start()

    each_peer(send_right)
    def wait_mid(sem):
        whole = mid.at[:, pl.ds(0, mid_n // yc_n * (yc_n - 1))]
        pltpu.make_async_copy(whole, whole, sem).wait()

    wait_mid(recv_sem.at[3])
    for dx in (1, 2, 3):
        cross_copy(dx).start()
    left[pl.ds(mid_low, mid_n), my_rows] = mid[0]

    def wait_direct(sem):
        whole = lstage.at[pl.ds(1, plane_n - 1), pl.ds(0, near_pieces)]
        pltpu.make_async_copy(whole, whole, sem).wait()

    wait_direct(recv_sem.at[1])
    for dx in (1, 2, 3):
        cross_copy(dx).wait_recv()
    wait_all(rstage, recv_sem.at[2])

    lane = lax.broadcasted_iota(jnp.int32, (width, width), 1) // quarter

    def product_second(o):
        acc = jnp.zeros((width, width), F32)
        for t in range(0, terms, 2):
            a_parts, b_parts = [], []
            for u in (t, t + 1):
                lefts = [left[stab[j, u, 0, o]] for j in range(4)]
                low = jnp.where(lane == 0, lefts[0], lefts[1])
                high = jnp.where(lane == 2, lefts[2], lefts[3])
                a_parts.append(jnp.where(lane < 2, low, high))
                b_parts += [right[stab[j, u, 1, o]] for j in range(4)]
            a = jnp.concatenate(a_parts, axis=1)
            b = jnp.concatenate(b_parts, axis=0)
            acc = acc + jnp.dot(a, b, preferred_element_type=F32)
        part2[o] = acc.astype(BF)

    def finish_second(span, h, total):
        own = x_ref[span, rows_of(lay, h)].astype(F32)
        out_ref[span, pl.ds(h * ROWS, ROWS)] = (1.5 * own - 0.5 * total).astype(BF)

    drain_second = reduce_rows(
        1, 4, product_second, part2, rs2, comb2, lambda: None, finish_second
    )

    lax.fori_loop(0, CHUNKS, drain_first, 0)
    lax.fori_loop(0, CHUNKS, drain_second, 0)
    for k in range(1, reach + 1):
        for up, s in hops():
            hop(up, k, s).wait_send()
    for step in range(1, 4):
        tab_copy(step).wait_send()
        row_copy(step).wait_send()
    for step in near:
        rows_copy(step).wait_send()
    for seg in parts:
        for up in both:
            far_copy(far_out, far_in, 0, up, seg).wait_send()
            far_copy(lfar_out, lfar_in, 1, up, seg).wait_send()
    wait_plane(first, send_sem.at[0])
    wait_direct(send_sem.at[1])
    wait_mid(send_sem.at[3])
    for dx in (1, 2, 3):
        cross_copy(dx).wait_send()
    wait_all(rstage, send_sem.at[2])


def local(
    y_n,
    x_blocks,
    send_first,
    send_left,
    send_right,
    terms_first,
    terms_second,
    live_first,
    live_second,
):
    grid_n = lax.axis_size("grid")
    blocks, width = x_blocks.shape[0], x_blocks.shape[1]
    count = terms_first.shape[2]
    quarter = width // 4
    yc_n = 2 * y_n
    z_n = grid_n // yc_n

    reach = z_n // 4
    steps = z_n // 2 - reach
    near_n = 2 * reach + 1

    def by_term(table):
        return table.reshape(blocks, count, 2).transpose(1, 2, 0)

    small = (
        send_first.reshape(1, grid_n),
        send_left.reshape(1, grid_n),
        send_right.reshape(1, grid_n),
        by_term(terms_first),
        by_term(terms_second),
        live_first.reshape(1, blocks),
        live_second.reshape(1, blocks),
    )
    share = jax.ShapeDtypeStruct((blocks, quarter, width), BF)
    vmem = pl.BlockSpec(memory_space=pltpu.VMEM)
    smem = pl.BlockSpec(memory_space=pltpu.SMEM)
    dma = pltpu.SemaphoreType.DMA
    return pl.pallas_call(
        functools.partial(kernel, grid_n, y_n, blocks, count),
        out_shape=(share, share),
        in_specs=[pl.BlockSpec(memory_space=pl.ANY), vmem, vmem, smem, vmem, vmem, vmem, vmem],
        out_specs=(vmem, vmem),
        scratch_shapes=[
            pltpu.VMEM((blocks, width, width), BF),
            *[pltpu.VMEM((blocks, quarter, width), BF)] * near_n,
            pltpu.VMEM((yc_n * 4, near_n, quarter, width), BF),
            pltpu.VMEM((yc_n * 4, near_n, quarter, width), BF),
            pltpu.VMEM((2, steps, yc_n * 4, quarter, width), BF),
            pltpu.VMEM((z_n - near_n, yc_n * 4, quarter, width), BF),
            pltpu.VMEM((2, steps, yc_n * 4, quarter, width), BF),
            pltpu.VMEM((z_n - near_n, yc_n * 4, quarter, width), BF),
            pltpu.VMEM((4, grid_n - (2 * reach - 1) * yc_n, quarter, width), BF),
            pltpu.VMEM((grid_n, quarter, width), BF),
            pltpu.VMEM((grid_n + 1, width, width), BF),
            pltpu.VMEM((grid_n + 1, width, width), BF),
            pltpu.VMEM((grid_n, quarter, width), BF),
            pltpu.VMEM((blocks, width, width), BF),
            pltpu.VMEM((blocks, width, width), BF),
            pltpu.VMEM((6, blocks, ROWS, width), BF),
            pltpu.VMEM((6, blocks, ROWS, width), BF),
            pltpu.VMEM((2, blocks, ROWS, width), BF),
            pltpu.VMEM((2, blocks, ROWS, width), BF),
            pltpu.VMEM((count, 2, 128), jnp.int32),
            pltpu.SMEM((count, 2, 128), jnp.int32),
            pltpu.VMEM((4, count, 2, 128), jnp.int32),
            pltpu.SMEM((4, count, 2, 128), jnp.int32),
            pltpu.VMEM((near_n, 4, 1, 128), jnp.int32),
            pltpu.SMEM((near_n, 4, 1, 128), jnp.int32),
            dma((4,)),
            dma((4,)),
            dma((2, reach, SUBS)),
            dma((2, reach, SUBS)),
            dma((2, 2, 2 * steps - 1)),
            dma((2, 2, 2 * steps - 1)),
            dma((3,)),
            dma((3,)),
            dma((3,)),
            dma((3,)),
            dma((2 + z_n,)),
            dma((2 + z_n,)),
            dma((3,)),
            dma((2, 6, CHUNKS)),
            dma((2, 6, CHUNKS)),
        ],
        compiler_params=pltpu.CompilerParams(
            collective_id=0, has_side_effects=True, vmem_limit_bytes=60 * 1024 * 1024
        ),
    )(x_blocks, *small)


def solution(mesh, y_n=4):
    return jax.shard_map(
        functools.partial(local, y_n),
        mesh=mesh,
        in_specs=(
            P("grid", None, None),
            P("grid", "layer", None, None),
            P("grid", "layer", None, None),
            P("grid", None, None),
            P("grid", "layer", None, None),
            P("grid", "layer", None, None),
            P("grid", "layer"),
            P("grid", "layer"),
        ),
        out_specs=(P("grid", "layer", None), P("grid", "layer", None)),
        check_vma=False,
    )
```

time: 159 us -> 137 us (0.86)
  Pallas kernels: 150 us -> 132 us
  other arithmetic: 3.04 us -> 0 us
    pallas_call x1, Pallas kernels: 150 us -> 132 us  [local(): pl.pallas_call(functools.partial(kernel, grid_n, y_n, blocks, count), out...]
    unnamed x4 -> x2, local copies, waits for them, and re-layouts: 3.18 us -> 3.74 us
where the time goes in v2:
time: 137 us; the launch traced here: 136 us
  Pallas kernels  132 us (96%)
  local copies, waits for them, and re-layouts  3.74 us (3%)
    pallas_call x1, Pallas kernels, local(): pl.pallas_call(functools.partial(kernel, grid_n, y_n, blocks, count), out...  132 us
    unnamed x2, local copies, waits for them, and re-layouts  3.74 us

profile of v2, /device:TPU:1, one launch (start us, length us, event | category | flops | bytes accessed | tf_op | source)
XLA Modules:
  0.0 136.1 jit_solution(8760126457040619122)
XLA Ops:
  0.6 131.7 %shard_map.95 = (bf16[64,32,128]{2,1,0:T(8,128)(2,1)}, bf16[64,32,128]{2,1,0:T(8,128)(2,1)}) custom-call(bf16[64,128,128]{2,1,0:T(8,128)(2,1)} %x_hbm.1, s32[1,64]{1,0:T(1,128)} %bitcast.13, s32[1,64]{1,0:T(1,128)} %bitcast.14, s32[1,64]{1,0:T(1,128)} %bitcast.15, s32[12,2,64]{2,1,0:T(2,128)} %bitcast.11, s32[12,2,64]{2,1,0:T(2,128)} %bitcast.12, ...), custom_call_target="tpu_custom_call" | custom-call | tf_op jit(solution)/shard_map/pallas_call | solution.py:720
  132.4 1.9 %copy.12 = bf16[64,32,128]{2,1,0:T(8,128)(2,1)} copy(bf16[64,32,128]{2,1,0:T(8,128)(2,1)} %get-tuple-element.4) | data formatting | bytes 1048576
  134.3 1.9 %copy.13 = bf16[64,32,128]{2,1,0:T(8,128)(2,1)} copy(bf16[64,32,128]{2,1,0:T(8,128)(2,1)} %get-tuple-element.5) | data formatting | bytes 1048576

commit v3 on v2

--- a/solution.py
+++ b/solution.py
@@ -13,6 +13,7 @@
 HALF = 64
 CHUNKS = 8
 LAG = 2
+DIRECT = 1
 FAR_FIRST = (4, 3, 5, 2, 6, 1, 7)
 ROWS = 16
 SUBS = 2
@@ -306,9 +307,8 @@
         each_mate(0, yc_n, one)
         dst[pl.ds(yc * z_n + low, count), my_rows] = src[0, pl.ds(low, count)]
 
-    def left_direct(k):
-        low, count = group(k)
-        for r in range(low, low + count):
+    def left_direct(pieces):
+        for r in pieces:
             slots = pl.ds(r * yc_n + yc, 1)
 
             def one(i, d, to):
@@ -465,7 +465,8 @@
         plane_send(stage, first, 0, k)
         fill_group(left_picks, lstage, k)
         if k < reach:
-            left_direct(k)
+            low, count = group(k)
+            left_direct(range(low, low + count))
     for seg in parts:
         fill_far(left_picks, lfar_out, seg)
     for seg in parts:
@@ -480,10 +481,11 @@
     for seg in parts:
         for up in both:
             far_copy(lfar_out, lfar_in, 1, up, seg).start()
-    near_pieces = 2 * reach - 1
+    near_pieces = 2 * reach - 1 + DIRECT
     mid_low = near_pieces * yc_n
     mid_n = grid_n - mid_low
-    for r in (0, 1):
+    left_direct(range(2 * reach - 1, near_pieces))
+    for r in range(2 - DIRECT):
         left_across(r, lambda m, r=r: lstage.at[pl.ds(m * 4, 4), near_pieces + r])
 
     def wait_all(src, sem):
@@ -501,7 +503,7 @@
     def rows_of(q, h):
         return pl.ds(pl.multiple_of(q * quarter + h * ROWS, ROWS), ROWS)
 
-    def reduce_rows(phase, together, product, src, got, comb, between, finish):
+    def reduce_rows(phase, together, product, src, got, comb, midway, between, finish):
         def copy(kind, c):
             span = pl.ds(c * per, per)
             if kind == 0:
@@ -547,12 +549,16 @@
             def _():
                 relay(c - LAG)
 
+            @pl.when(c == CHUNKS // 2 - 1)
+            def _():
+                midway()
+
             return carry
 
         lax.fori_loop(0, CHUNKS, chunk, 0)
-        between()
         for c in range(CHUNKS - LAG, CHUNKS):
             relay(c)
+        between()
 
         def close(c, carry):
             span = pl.ds(c * per, per)
@@ -592,9 +598,20 @@
             for up in both:
                 far_copy(lfar_out, lfar_in, 1, up, seg).wait_recv()
         for f in range(far_n):
-            left_across(2 + f, lambda m, f=f: lfar_in.at[f, pl.ds(m * 4, 4)])
-
-    drain_first = reduce_rows(0, 4, product_first, part, rs1, comb1, send_late, finish_first)
+            left_across(2 - DIRECT + f, lambda m, f=f: lfar_in.at[f, pl.ds(m * 4, 4)])
+
+    def wait_mid(sem):
+        whole = mid.at[:, pl.ds(0, mid_n // yc_n * (yc_n - 1))]
+        pltpu.make_async_copy(whole, whole, sem).wait()
+
+    def send_cross():
+        wait_mid(recv_sem.at[3])
+        for dx in (1, 2, 3):
+            cross_copy(dx).start()
+
+    drain_first = reduce_rows(
+        0, 4, product_first, part, rs1, comb1, send_late, lambda: None, finish_first
+    )
 
     def fill_right(i, d):
         rstage[i] = sq_ref[ssr[0, d]]
@@ -614,13 +631,7 @@
         ).start()
 
     each_peer(send_right)
-    def wait_mid(sem):
-        whole = mid.at[:, pl.ds(0, mid_n // yc_n * (yc_n - 1))]
-        pltpu.make_async_copy(whole, whole, sem).wait()
-
-    wait_mid(recv_sem.at[3])
-    for dx in (1, 2, 3):
-        cross_copy(dx).start()
+    send_cross()
     left[pl.ds(mid_low, mid_n), my_rows] = mid[0]
 
     def wait_direct(sem):
@@ -654,7 +665,7 @@
         out_ref[span, pl.ds(h * ROWS, ROWS)] = (1.5 * own - 0.5 * total).astype(BF)
 
     drain_second = reduce_rows(
-        1, 4, product_second, part2, rs2, comb2, lambda: None, finish_second
+        1, 4, product_second, part2, rs2, comb2, lambda: None, lambda: None, finish_second
     )
 
     lax.fori_loop(0, CHUNKS, drain_first, 0)
@@ -731,7 +742,7 @@
             pltpu.VMEM((z_n - near_n, yc_n * 4, quarter, width), BF),
             pltpu.VMEM((2, steps, yc_n * 4, quarter, width), BF),
             pltpu.VMEM((z_n - near_n, yc_n * 4, quarter, width), BF),
-            pltpu.VMEM((4, grid_n - (2 * reach - 1) * yc_n, quarter, width), BF),
+            pltpu.VMEM((4, grid_n - (2 * reach - 1 + DIRECT) * yc_n, quarter, width), BF),
             pltpu.VMEM((grid_n, quarter, width), BF),
             pltpu.VMEM((grid_n + 1, width, width), BF),
             pltpu.VMEM((grid_n + 1, width, width), BF),

time: 137 us -> 132 us (0.964)
  Pallas kernels: 132 us -> 127 us
    pallas_call x1, Pallas kernels: 132 us -> 127 us  [local(): pl.pallas_call(functools.partial(kernel, grid_n, y_n, blocks, count), out...]
where the time goes in v3:
time: 132 us
  Pallas kernels  127 us (96%)
  local copies, waits for them, and re-layouts  3.74 us (3%)
    pallas_call x1, Pallas kernels, local(): pl.pallas_call(functools.partial(kernel, grid_n, y_n, blocks, count), out...  127 us
    unnamed x2, local copies, waits for them, and re-layouts  3.74 us

profile of v3, /device:TPU:1, one launch (start us, length us, event | category | flops | bytes accessed | tf_op | source)
XLA Modules:
  0.0 131.6 jit_solution(7868843996659337282)
XLA Ops:
  0.6 127.2 %shard_map.95 = (bf16[64,32,128]{2,1,0:T(8,128)(2,1)}, bf16[64,32,128]{2,1,0:T(8,128)(2,1)}) custom-call(bf16[64,128,128]{2,1,0:T(8,128)(2,1)} %x_hbm.1, s32[1,64]{1,0:T(1,128)} %bitcast.13, s32[1,64]{1,0:T(1,128)} %bitcast.14, s32[1,64]{1,0:T(1,128)} %bitcast.15, s32[12,2,64]{2,1,0:T(2,128)} %bitcast.11, s32[12,2,64]{2,1,0:T(2,128)} %bitcast.12, ...), custom_call_target="tpu_custom_call" | custom-call | tf_op jit(solution)/shard_map/pallas_call | solution.py:731
  127.9 1.9 %copy.12 = bf16[64,32,128]{2,1,0:T(8,128)(2,1)} copy(bf16[64,32,128]{2,1,0:T(8,128)(2,1)} %get-tuple-element.4) | data formatting | bytes 1048576
  129.7 1.9 %copy.13 = bf16[64,32,128]{2,1,0:T(8,128)(2,1)} copy(bf16[64,32,128]{2,1,0:T(8,128)(2,1)} %get-tuple-element.5) | data formatting | bytes 1048576

commit v4 on v3

--- a/solution.py
+++ b/solution.py
@@ -24,30 +24,11 @@
     return 0 if k == 0 else (2 * k - 1 if 2 * k <= n else 2 * (n - k))
 
 
-def kernel(
-    grid_n,
-    y_n,
-    blocks,
-    terms,
-    x_hbm,
-    sf_ref,
-    sl_ref,
-    ssr,
-    tf_ref,
-    ts_ref,
-    lf_ref,
-    ls_ref,
-    sq_ref,
-    out_ref,
-    x_ref,
-    *refs,
-):
+def kernel(grid_n, y_n, blocks, terms, x_hbm, *refs):
     near_n = 2 * (grid_n // (2 * y_n) // 4) + 1
-    gathered = refs[:near_n]
-    run(
-        grid_n, y_n, blocks, terms, x_hbm, sf_ref, sl_ref, ssr, tf_ref, ts_ref, lf_ref, ls_ref,
-        sq_ref, out_ref, x_ref, gathered, *refs[near_n:]
-    )
+    small, outs, refs = refs[:7], refs[7:9], refs[9:]
+    held, x_ref, gathered, rest = refs[:7], refs[7], refs[8 : 8 + near_n], refs[8 + near_n :]
+    run(grid_n, y_n, blocks, terms, x_hbm, small, *held, *outs, x_ref, gathered, *rest)
 
 
 def run(
@@ -56,6 +37,7 @@
     blocks,
     terms,
     x_hbm,
+    small,
     sf_ref,
     sl_ref,
     ssr,
@@ -109,7 +91,13 @@
     me = lax.axis_index("grid")
     lay = lax.axis_index("layer")
     load_x = pltpu.make_async_copy(x_hbm, x_ref, loc_sem.at[0])
-    load_x.start()
+    held = (sf_ref, sl_ref, ssr, tf_ref, ts_ref, lf_ref, ls_ref)
+    loads = [
+        pltpu.make_async_copy(src, dst, loc_sem.at[3 + n])
+        for n, (src, dst) in enumerate(zip(small, held))
+    ]
+    for load in (*loads, load_x):
+        load.start()
     width = x_ref.shape[1]
     quarter = width // 4
     z_n = grid_n // (2 * y_n)
@@ -176,6 +164,8 @@
         return carry
 
     lax.fori_loop(0, yc_n, greet_layers, 0)
+    for load in loads:
+        load.wait()
 
     def moved(slots):
         away = lax.rem(lax.div(slots, yc_n) - z + z_n, z_n)
@@ -503,7 +493,7 @@
     def rows_of(q, h):
         return pl.ds(pl.multiple_of(q * quarter + h * ROWS, ROWS), ROWS)
 
-    def reduce_rows(phase, together, product, src, got, comb, midway, between, finish):
+    def reduce_rows(phase, together, product, src, got, comb, midway, finish):
         def copy(kind, c):
             span = pl.ds(c * per, per)
             if kind == 0:
@@ -556,10 +546,6 @@
             return carry
 
         lax.fori_loop(0, CHUNKS, chunk, 0)
-        for c in range(CHUNKS - LAG, CHUNKS):
-            relay(c)
-        between()
-
         def close(c, carry):
             span = pl.ds(c * per, per)
             for h, direct, joined in ((0, 3, 4), (1, 2, 5)):
@@ -573,7 +559,11 @@
                 finish(span, h, total)
             return carry
 
-        lax.fori_loop(0, CHUNKS, close, 0)
+        for c in range(CHUNKS - LAG, CHUNKS):
+            if c == CHUNKS - 1:
+                lax.fori_loop(0, CHUNKS // 2, close, 0)
+            relay(c)
+        lax.fori_loop(CHUNKS // 2, CHUNKS, close, 0)
 
         def drain(c, carry):
             for kind in range(6):
@@ -610,17 +600,11 @@
             cross_copy(dx).start()
 
     drain_first = reduce_rows(
-        0, 4, product_first, part, rs1, comb1, send_late, lambda: None, finish_first
+        0, 4, product_first, part, rs1, comb1, send_late, finish_first
     )
 
-    def fill_right(i, d):
+    def send_right(i, d):
         rstage[i] = sq_ref[ssr[0, d]]
-
-    rstage[0] = sq_ref[ssr[0, me]]
-    each_peer(fill_right)
-    right[me] = rstage[0]
-
-    def send_right(i, d):
         pltpu.make_async_remote_copy(
             src_ref=rstage.at[i],
             dst_ref=right.at[me],
@@ -631,6 +615,7 @@
         ).start()
 
     each_peer(send_right)
+    right[me] = sq_ref[ssr[0, me]]
     send_cross()
     left[pl.ds(mid_low, mid_n), my_rows] = mid[0]
 
@@ -665,7 +650,7 @@
         out_ref[span, pl.ds(h * ROWS, ROWS)] = (1.5 * own - 0.5 * total).astype(BF)
 
     drain_second = reduce_rows(
-        1, 4, product_second, part2, rs2, comb2, lambda: None, lambda: None, finish_second
+        1, 8, product_second, part2, rs2, comb2, lambda: None, finish_second
     )
 
     lax.fori_loop(0, CHUNKS, drain_first, 0)
@@ -726,14 +711,20 @@
     )
     share = jax.ShapeDtypeStruct((blocks, quarter, width), BF)
     vmem = pl.BlockSpec(memory_space=pltpu.VMEM)
-    smem = pl.BlockSpec(memory_space=pltpu.SMEM)
     dma = pltpu.SemaphoreType.DMA
     return pl.pallas_call(
         functools.partial(kernel, grid_n, y_n, blocks, count),
         out_shape=(share, share),
-        in_specs=[pl.BlockSpec(memory_space=pl.ANY), vmem, vmem, smem, vmem, vmem, vmem, vmem],
+        in_specs=[pl.BlockSpec(memory_space=pl.ANY)] * 8,
         out_specs=(vmem, vmem),
         scratch_shapes=[
+            pltpu.VMEM((1, grid_n), jnp.int32),
+            pltpu.VMEM((1, grid_n), jnp.int32),
+            pltpu.SMEM((1, grid_n), jnp.int32),
+            pltpu.VMEM((count, 2, blocks), jnp.int32),
+            pltpu.VMEM((count, 2, blocks), jnp.int32),
+            pltpu.VMEM((1, blocks), jnp.int32),
+            pltpu.VMEM((1, blocks), jnp.int32),
             pltpu.VMEM((blocks, width, width), BF),
             *[pltpu.VMEM((blocks, quarter, width), BF)] * near_n,
             pltpu.VMEM((yc_n * 4, near_n, quarter, width), BF),
@@ -771,7 +762,7 @@
             dma((3,)),
             dma((2 + z_n,)),
             dma((2 + z_n,)),
-            dma((3,)),
+            dma((10,)),
             dma((2, 6, CHUNKS)),
             dma((2, 6, CHUNKS)),
         ],

time: 132 us -> 130 us (0.985)
    pallas_call x1, Pallas kernels: 127 us -> 126 us  [local(): pl.pallas_call(functools.partial(kernel, grid_n, y_n, blocks, count), out...]
where the time goes in v4:
time: 130 us
  Pallas kernels  126 us (97%)
  local copies, waits for them, and re-layouts  3.74 us (3%)
    pallas_call x1, Pallas kernels, local(): pl.pallas_call(functools.partial(kernel, grid_n, y_n, blocks, count), out...  126 us
    unnamed x2, local copies, waits for them, and re-layouts  3.74 us

profile of v4, /device:TPU:1, one launch (start us, length us, event | category | flops | bytes accessed | tf_op | source)
XLA Modules:
  0.0 130.2 jit_solution(8694090792615974558)
XLA Ops:
  0.6 125.8 %shard_map.95 = (bf16[64,32,128]{2,1,0:T(8,128)(2,1)}, bf16[64,32,128]{2,1,0:T(8,128)(2,1)}) custom-call(bf16[64,128,128]{2,1,0:T(8,128)(2,1)} %x_hbm.1, s32[1,64]{1,0:T(1,128)} %bitcast.13, s32[1,64]{1,0:T(1,128)} %bitcast.14, s32[1,64]{1,0:T(1,128)} %bitcast.15, s32[12,2,64]{2,1,0:T(2,128)} %bitcast.11, s32[12,2,64]{2,1,0:T(2,128)} %bitcast.12, ...), custom_call_target="tpu_custom_call" | custom-call | tf_op jit(solution)/shard_map/pallas_call | solution.py:715
  126.5 1.9 %copy.12 = bf16[64,32,128]{2,1,0:T(8,128)(2,1)} copy(bf16[64,32,128]{2,1,0:T(8,128)(2,1)} %get-tuple-element.4) | data formatting | bytes 1048576
  128.3 1.9 %copy.13 = bf16[64,32,128]{2,1,0:T(8,128)(2,1)} copy(bf16[64,32,128]{2,1,0:T(8,128)(2,1)} %get-tuple-element.5) | data formatting | bytes 1048576

commit v5 on v4

--- a/solution.py
+++ b/solution.py
@@ -13,7 +13,7 @@
 HALF = 64
 CHUNKS = 8
 LAG = 2
-DIRECT = 1
+DIRECT = 0
 FAR_FIRST = (4, 3, 5, 2, 6, 1, 7)
 ROWS = 16
 SUBS = 2
@@ -314,15 +314,15 @@
             each_mate(0, yc_n, one)
             left[slots, my_rows] = lstage[0, pl.ds(r, 1)]
 
-    def left_across(piece, src_of):
+    def left_across(piece, which, src_of):
         slot = piece * yc_n + yc
 
         def one(m, carry):
             pltpu.make_async_remote_copy(
                 src_ref=src_of(m),
                 dst_ref=mid.at[:, slot],
-                send_sem=send_sem.at[3],
-                recv_sem=recv_sem.at[3],
+                send_sem=send_sem.at[which],
+                recv_sem=recv_sem.at[which],
                 device_id=(zs[0] + mate_yc(m), lay),
                 device_id_type=MESH,
             ).start()
@@ -331,12 +331,14 @@
         lax.fori_loop(1, yc_n, one, 0)
         mid[:, slot] = src_of(0)[...]
 
-    def cross_copy(dx):
+    def cross_copy(dx, part_of):
+        early = (2 - DIRECT) * yc_n
+        low, count = ((0, early), (early, mid_n - early))[part_of]
         return pltpu.make_async_remote_copy(
-            src_ref=mid.at[dx],
-            dst_ref=left.at[pl.ds(mid_low, mid_n), my_rows],
-            send_sem=cross_send.at[dx - 1],
-            recv_sem=cross_recv.at[dx - 1],
+            src_ref=mid.at[dx, pl.ds(low, count)],
+            dst_ref=left.at[pl.ds(mid_low + low, count), my_rows],
+            send_sem=cross_send.at[part_of, dx - 1],
+            recv_sem=cross_recv.at[part_of, dx - 1],
             device_id=(me, lays[dx]),
             device_id_type=MESH,
         )
@@ -476,7 +478,7 @@
     mid_n = grid_n - mid_low
     left_direct(range(2 * reach - 1, near_pieces))
     for r in range(2 - DIRECT):
-        left_across(r, lambda m, r=r: lstage.at[pl.ds(m * 4, 4), near_pieces + r])
+        left_across(r, 3, lambda m, r=r: lstage.at[pl.ds(m * 4, 4), near_pieces + r])
 
     def wait_all(src, sem):
         whole = src.at[pl.ds(1, src.shape[0] - 1)]
@@ -493,7 +495,7 @@
     def rows_of(q, h):
         return pl.ds(pl.multiple_of(q * quarter + h * ROWS, ROWS), ROWS)
 
-    def reduce_rows(phase, together, product, src, got, comb, midway, finish):
+    def reduce_rows(phase, together, product, src, got, comb, midway, between, finish):
         def copy(kind, c):
             span = pl.ds(c * per, per)
             if kind == 0:
@@ -539,7 +541,7 @@
             def _():
                 relay(c - LAG)
 
-            @pl.when(c == CHUNKS // 2 - 1)
+            @pl.when(c == 1)
             def _():
                 midway()
 
@@ -563,6 +565,7 @@
             if c == CHUNKS - 1:
                 lax.fori_loop(0, CHUNKS // 2, close, 0)
             relay(c)
+        between()
         lax.fori_loop(CHUNKS // 2, CHUNKS, close, 0)
 
         def drain(c, carry):
@@ -588,19 +591,20 @@
             for up in both:
                 far_copy(lfar_out, lfar_in, 1, up, seg).wait_recv()
         for f in range(far_n):
-            left_across(2 - DIRECT + f, lambda m, f=f: lfar_in.at[f, pl.ds(m * 4, 4)])
-
-    def wait_mid(sem):
-        whole = mid.at[:, pl.ds(0, mid_n // yc_n * (yc_n - 1))]
+            left_across(2 - DIRECT + f, 4, lambda m, f=f: lfar_in.at[f, pl.ds(m * 4, 4)])
+
+    def wait_mid(part_of, sem):
+        pieces = (2 - DIRECT, far_n)[part_of]
+        whole = mid.at[:, pl.ds(0, pieces * (yc_n - 1))]
         pltpu.make_async_copy(whole, whole, sem).wait()
 
-    def send_cross():
-        wait_mid(recv_sem.at[3])
+    def send_cross(part_of):
+        wait_mid(part_of, recv_sem.at[3 + part_of])
         for dx in (1, 2, 3):
-            cross_copy(dx).start()
+            cross_copy(dx, part_of).start()
 
     drain_first = reduce_rows(
-        0, 4, product_first, part, rs1, comb1, send_late, finish_first
+        0, 4, product_first, part, rs1, comb1, send_late, lambda: send_cross(0), finish_first
     )
 
     def send_right(i, d):
@@ -616,7 +620,7 @@
 
     each_peer(send_right)
     right[me] = sq_ref[ssr[0, me]]
-    send_cross()
+    send_cross(1)
     left[pl.ds(mid_low, mid_n), my_rows] = mid[0]
 
     def wait_direct(sem):
@@ -625,7 +629,8 @@
 
     wait_direct(recv_sem.at[1])
     for dx in (1, 2, 3):
-        cross_copy(dx).wait_recv()
+        cross_copy(dx, 0).wait_recv()
+        cross_copy(dx, 1).wait_recv()
     wait_all(rstage, recv_sem.at[2])
 
     lane = lax.broadcasted_iota(jnp.int32, (width, width), 1) // quarter
@@ -650,7 +655,7 @@
         out_ref[span, pl.ds(h * ROWS, ROWS)] = (1.5 * own - 0.5 * total).astype(BF)
 
     drain_second = reduce_rows(
-        1, 8, product_second, part2, rs2, comb2, lambda: None, finish_second
+        1, 8, product_second, part2, rs2, comb2, lambda: None, lambda: None, finish_second
     )
 
     lax.fori_loop(0, CHUNKS, drain_first, 0)
@@ -669,9 +674,11 @@
             far_copy(lfar_out, lfar_in, 1, up, seg).wait_send()
     wait_plane(first, send_sem.at[0])
     wait_direct(send_sem.at[1])
-    wait_mid(send_sem.at[3])
+    wait_mid(0, send_sem.at[3])
+    wait_mid(1, send_sem.at[4])
     for dx in (1, 2, 3):
-        cross_copy(dx).wait_send()
+        cross_copy(dx, 0).wait_send()
+        cross_copy(dx, 1).wait_send()
     wait_all(rstage, send_sem.at[2])
 
 
@@ -750,14 +757,14 @@
             pltpu.SMEM((4, count, 2, 128), jnp.int32),
             pltpu.VMEM((near_n, 4, 1, 128), jnp.int32),
             pltpu.SMEM((near_n, 4, 1, 128), jnp.int32),
-            dma((4,)),
-            dma((4,)),
+            dma((5,)),
+            dma((5,)),
             dma((2, reach, SUBS)),
             dma((2, reach, SUBS)),
             dma((2, 2, 2 * steps - 1)),
             dma((2, 2, 2 * steps - 1)),
-            dma((3,)),
-            dma((3,)),
+            dma((2, 3)),
+            dma((2, 3)),
             dma((3,)),
             dma((3,)),
             dma((2 + z_n,)),

time: 130 us -> 130 us (level)
  no operation moved by 1% of the time
where the time goes in v5:
time: 130 us
  Pallas kernels  126 us (97%)
  local copies, waits for them, and re-layouts  3.74 us (3%)
    pallas_call x1, Pallas kernels, local(): pl.pallas_call(functools.partial(kernel, grid_n, y_n, blocks, count), out...  126 us
    unnamed x2, local copies, waits for them, and re-layouts  3.74 us

profile of v5, /device:TPU:1, one launch (start us, length us, event | category | flops | bytes accessed | tf_op | source)
XLA Modules:
  0.0 130.2 jit_solution(3365463180575560226)
XLA Ops:
  0.6 125.8 %shard_map.95 = (bf16[64,32,128]{2,1,0:T(8,128)(2,1)}, bf16[64,32,128]{2,1,0:T(8,128)(2,1)}) custom-call(bf16[64,128,128]{2,1,0:T(8,128)(2,1)} %x_hbm.1, s32[1,64]{1,0:T(1,128)} %bitcast.13, s32[1,64]{1,0:T(1,128)} %bitcast.14, s32[1,64]{1,0:T(1,128)} %bitcast.15, s32[12,2,64]{2,1,0:T(2,128)} %bitcast.11, s32[12,2,64]{2,1,0:T(2,128)} %bitcast.12, ...), custom_call_target="tpu_custom_call" | custom-call | tf_op jit(solution)/shard_map/pallas_call | solution.py:722
  126.5 1.9 %copy.12 = bf16[64,32,128]{2,1,0:T(8,128)(2,1)} copy(bf16[64,32,128]{2,1,0:T(8,128)(2,1)} %get-tuple-element.4) | data formatting | bytes 1048576
  128.3 1.9 %copy.13 = bf16[64,32,128]{2,1,0:T(8,128)(2,1)} copy(bf16[64,32,128]{2,1,0:T(8,128)(2,1)} %get-tuple-element.5) | data formatting | bytes 1048576
